TPU v7x, 32 devices: a whole 2x2x4 slice. The times are simulated.
32 devices in a mesh: grp: 2 (over x), tok: 8 (over z, y), ep: 2 (over core).
Axes of the slice: x: 2, y: 2, z: 4, core: 2. Of those that a mesh axis runs over, the one named last changes fastest.
Arguments:
- tokens: bfloat16 [2, 2048, 768], P('ep', ('grp', 'tok')), parts along dimension 1, may hold values from -6 to 6
- norm_gain: float32 [768], replicated, may hold values from 0.5 to 1.5
- query_weight: bfloat16 [768, 768], replicated, may hold values from -0.21875 to 0.21875
- w_key: bfloat16 [768, 768], replicated, may hold values from -0.21875 to 0.21875
- w_value: bfloat16 [768, 768], replicated, may hold values from -0.21875 to 0.21875
- w_out: bfloat16 [768, 768], replicated, may hold values from -0.21875 to 0.21875
- head_scale: float32 [12], replicated, may hold values from 0.5 to 64
- matching: int32 [2, 64], P('ep', ('grp', 'tok')), parts along dimension 1, may hold values from 0 to 3, as said below
- valid: int32 [2, 64], P('ep', ('grp', 'tok')), parts along dimension 1, may hold values from 1 to 32, as said below
- stops: int32 [2, 16, 4], P('ep', ('grp', 'tok')), parts along dimension 1, may hold values from 0 to 7, as said below
Outputs:
- refined: bfloat16 [2, 2048, 768], P('ep', ('grp', 'tok')), parts along dimension 1
There are 2 independent parts, one for each index of `grp`. A program takes and returns all parts, laid end to end along the dimension named above; an argument that names none is the same for every part. Nothing has to cross between parts.
Inputs may be any that keep to these rules, and one draw needn't show every extreme that they name: `matching`: each aligned group of 4 entries is a permutation of 0 to 3. `valid`: in every block of 4 tiles one tile is full. `stops`: the 4 entries of block t are distinct blocks within 3 of t, and one of them is t - 3 or t + 3.
All inputs are finite; a program needn't handle non-finite values.
Results may differ from a plain program's by a relative error of at most 0.004.
The roundings to bfloat16 on the way count: a program that leaves them out, or rounds other values in their place, can miss the bound.
Values may be sent and summed in bfloat16 or wider, within the bound.
A program may use at most 64 MiB of HBM per device.

v0:
```python
import math

import jax
import jax.numpy as jnp
import numpy as np
from jax import lax
from jax.experimental import pallas as pl
from jax.experimental.pallas import tpu as pltpu
from jax.sharding import PartitionSpec as P

BAND = 3
ROW_PATCHES = 1024
LANES = 128
META = 16
MESH = pl.DeviceIdType.MESH
LOG2E = 1.4426950408889634


def rotary_table(blocks, rows, head_dim):
    quarter = head_dim // 4
    spots = np.arange(-BAND * rows, (blocks + BAND) * rows, dtype=np.int32)
    freqs = np.float32(100.0) ** (-np.arange(quarter, dtype=np.float32) / np.float32(quarter))
    parts = []
    for coordinate in (spots // ROW_PATCHES, spots % ROW_PATCHES):
        angle = coordinate.astype(np.float32)[:, None] * freqs[None, :].astype(np.float32)
        parts.append((np.cos(angle), np.sin(angle)))
    cosine = np.concatenate([half for c, _ in parts for half in (c, c)], axis=1)
    sine = np.concatenate([half for _, s in parts for half in (-s, s)], axis=1)
    copies = LANES // head_dim
    table = np.concatenate([cosine] * copies + [sine] * copies, axis=1)
    return table.reshape(blocks + 2 * BAND, rows, 2 * LANES).astype(np.float32)


def make_kernel(blocks, rows, width, heads, tiles):
    head_dim = width // heads
    quarter = head_dim // 4
    tile_rows = rows // tiles
    chunks = width // LANES
    per_chunk = LANES // head_dim
    slots = 2 * BAND + 1

    def turned(values, cosine, sine):
        lane = lax.broadcasted_iota(jnp.int32, values.shape, 1)
        ahead = pltpu.roll(values, LANES - quarter, 1)
        behind = pltpu.roll(values, quarter, 1)
        other = jnp.where(lane % (2 * quarter) < quarter, ahead, behind)
        return values * cosine + other * sine

    def kernel(
        tok_ref, gain_ref, scale_ref, match_ref, valid_ref, stops_ref,
        wq_hbm, wk_hbm, wv_hbm, wo_hbm, table_hbm,
        out_ref,
        wq, wk, wv, wo, table, mine, buf, match_out, match_in,
        queries, keys, values, masks, attended,
        local_sem, send_sem, recv_sem, match_sem,
    ):
        t = lax.axis_index("tok")
        ep = lax.axis_index("ep")
        other_ep = 1 - ep
        s = 1 - 2 * (t % 2)

        def there(k):
            spot = t + s * k
            return (spot >= 0) & (spot < blocks)

        def count(k):
            return there(k).astype(jnp.int32)

        loads = [
            pltpu.make_async_copy(table_hbm.at[pl.ds(t, slots)], table, local_sem.at[0]),
            pltpu.make_async_copy(wq_hbm, wq, local_sem.at[1]),
            pltpu.make_async_copy(wk_hbm, wk, local_sem.at[2]),
            pltpu.make_async_copy(wv_hbm, wv, local_sem.at[3]),
            pltpu.make_async_copy(wo_hbm, wo, local_sem.at[4]),
        ]

        barrier = pltpu.get_barrier_semaphore()

        def greet(tok, e):
            pl.semaphore_signal(
                barrier, inc=1, device_id={"tok": tok, "ep": e}, device_id_type=MESH
            )

        greet(t, other_ep)
        greet(t + s, ep)
        greet(t + s, other_ep)
        for k in (2, -2):
            @pl.when(there(k))
            def _():
                greet(t + s * k, ep)
                greet(t + s * k, other_ep)

        for load in loads:
            load.start()

        floated = tok_ref[0].astype(jnp.float32)
        center = jnp.mean(floated, axis=-1, keepdims=True)
        apart = floated - center
        spread = jnp.mean(apart * apart, axis=-1, keepdims=True)
        mine[:rows, :] = (apart * lax.rsqrt(spread + 1e-05) * gain_ref[...]).astype(jnp.bfloat16)

        row = lax.broadcasted_iota(jnp.int32, (8, LANES), 0)
        matched = jnp.zeros((8, LANES), jnp.float32)
        lane = lax.broadcasted_iota(jnp.int32, (8, rows), 1)
        live = jnp.zeros((8, rows), jnp.int32)
        for j in range(tiles):
            matched = jnp.where(row == j, match_ref[0, j].astype(jnp.float32), matched)
            live = jnp.where(lane // tile_rows == j, valid_ref[0, j], live)
        match_out[...] = matched
        hidden = jnp.where(lane % tile_rows < live, jnp.float32(0), jnp.float32(-1e30))

        pl.semaphore_wait(barrier, 3 + 2 * count(2) + 2 * count(-2))

        swap = pltpu.make_async_remote_copy(
            match_out, match_in, match_sem.at[0], match_sem.at[1],
            device_id={"tok": t, "ep": other_ep}, device_id_type=MESH,
        )
        swap.start()

        def transfer(src, number, slot, tok, e):
            return pltpu.make_async_remote_copy(
                src, buf.at[slot], send_sem.at[number], recv_sem.at[slot],
                device_id={"tok": tok, "ep": e}, device_id_type=MESH,
            )

        mid = BAND
        direct = [
            (2, transfer(mine, 0, mid - 2 * s, t + 2 * s, other_ep)),
            (-2, transfer(mine, 1, mid + 2 * s, t - 2 * s, other_ep)),
            (1, transfer(mine, 2, mid - s, t + s, other_ep)),
            (0, transfer(mine, 3, mid, t, other_ep)),
        ]
        relay_far = transfer(buf.at[mid + s], 4, mid + 3 * s, t - 2 * s, ep)
        relay_side = transfer(buf.at[mid + 2 * s], 5, mid + s, t + s, ep)
        relay_last = transfer(buf.at[mid - s], 6, mid - 3 * s, t + 2 * s, ep)
        last_there = there(2) & there(-1)

        def arrived(k):
            transfer(mine, 0, mid + s * k, t + s, other_ep).wait_recv()

        mine[rows:, :] = jnp.zeros((META, width), jnp.bfloat16)
        swap.wait_recv()
        mine[rows:, :LANES] = jnp.concatenate([match_in[...], hidden], axis=0).astype(jnp.bfloat16)
        for k, copy in direct:
            if k in (2, -2):
                pl.when(there(k))(copy.start)
            else:
                copy.start()

        loads[0].wait()
        loads[1].wait()
        own = mine[:rows, :]
        own_cos = table[mid, :, :LANES]
        own_sin = table[mid, :, LANES:]
        for pair in range(0, chunks, 2):
            wide = pl.ds(pair * LANES, 2 * LANES)
            product = jnp.dot(own, wq[:, wide], preferred_element_type=jnp.float32)
            for c in range(2):
                queries[:, pl.ds((pair + c) * LANES, LANES)] = turned(
                    product[:, c * LANES : (c + 1) * LANES], own_cos, own_sin
                ).astype(jnp.bfloat16)
        loads[2].wait()
        loads[3].wait()

        def project(k):
            slot = mid + s * k
            source = buf[slot, :rows, :]
            meta = buf[slot, rows:, :LANES].astype(jnp.float32)
            masks[slot] = meta[8:, :]
            cos_parts, sin_parts = [], []
            for g in range(tiles):
                picked = table[slot, 0:tile_rows, :]
                for j in range(1, tiles):
                    hit = jnp.broadcast_to(
                        jnp.concatenate([meta[j : j + 1, :]] * 2, axis=1) == g,
                        (tile_rows, 2 * LANES),
                    )
                    picked = jnp.where(
                        hit, table[slot, j * tile_rows : (j + 1) * tile_rows, :], picked
                    )
                cos_parts.append(picked[:, :LANES])
                sin_parts.append(picked[:, LANES:])
            cosine = jnp.concatenate(cos_parts, axis=0)
            sine = jnp.concatenate(sin_parts, axis=0)
            for pair in range(0, chunks, 2):
                wide = pl.ds(pair * LANES, 2 * LANES)
                product = jnp.dot(source, wk[:, wide], preferred_element_type=jnp.float32)
                for c in range(2):
                    keys[slot, :, pl.ds((pair + c) * LANES, LANES)] = turned(
                        product[:, c * LANES : (c + 1) * LANES], cosine, sine
                    ).astype(jnp.bfloat16)
                values[slot, :, wide] = jnp.dot(
                    source, wv[:, wide], preferred_element_type=jnp.float32
                ).astype(jnp.bfloat16)

        arrived(0)
        project(0)
        arrived(1)
        pl.when(there(-2))(relay_far.start)

        @pl.when(there(2))
        def _():
            arrived(2)
            relay_side.start()

        project(1)

        @pl.when(there(-2))
        def _():
            arrived(-2)

        @pl.when(there(2))
        def _():
            project(2)

        @pl.when(there(-1))
        def _():
            arrived(-1)

        pl.when(last_there)(relay_last.start)

        @pl.when(there(-2))
        def _():
            project(-2)

        @pl.when(there(-1))
        def _():
            project(-1)

        for k in (3, -3):
            @pl.when(there(k))
            def _():
                arrived(k)
                project(k)

        picks = [
            jnp.clip(stops_ref[0, 0, i] - t + BAND, 0, slots - 1) for i in range(stops_ref.shape[2])
        ]
        mask = jnp.concatenate([masks[p][0:1, :] for p in picks], axis=1)
        lane_of = lax.broadcasted_iota(jnp.int32, (rows, LANES), 1)
        for c in range(chunks):
            span = pl.ds(c * LANES, LANES)
            ask = queries[:, span]
            nothing = jnp.zeros_like(ask)
            asked = jnp.concatenate(
                [
                    jnp.where(lane_of // head_dim == h, ask, nothing)
                    for h in range(per_chunk)
                ],
                axis=0,
            )
            key_use = jnp.concatenate([keys[p, :, span] for p in picks], axis=0)
            value_use = jnp.concatenate([values[p, :, span] for p in picks], axis=0)
            raw = lax.dot_general(
                asked, key_use, (((1,), (1,)), ((), ())), preferred_element_type=jnp.float32
            )
            weights, totals = [], []
            for h in range(per_chunk):
                factor = scale_ref[c * per_chunk + h] * jnp.float32(LOG2E / math.sqrt(head_dim))
                scores = raw[h * rows : (h + 1) * rows] * factor + mask
                best = jnp.max(scores, axis=1, keepdims=True)
                weight = jnp.exp2(scores - best)
                totals.append(jnp.sum(weight, axis=1, keepdims=True))
                weights.append(weight.astype(jnp.bfloat16))
            summed = jnp.dot(
                jnp.concatenate(weights, axis=0), value_use, preferred_element_type=jnp.float32
            )
            result = summed[:rows] / totals[0]
            for h in range(1, per_chunk):
                result = jnp.where(
                    lane_of // head_dim == h, summed[h * rows : (h + 1) * rows] / totals[h], result
                )
            attended[:, span] = result.astype(jnp.bfloat16)

        loads[4].wait()
        for pair in range(0, chunks, 2):
            wide = pl.ds(pair * LANES, 2 * LANES)
            mixed = jnp.dot(attended[...], wo[:, wide], preferred_element_type=jnp.float32)
            out_ref[0, :, wide] = (
                tok_ref[0, :, wide].astype(jnp.float32) + mixed
            ).astype(jnp.bfloat16)

        swap.wait_send()
        for k, copy in direct:
            if k in (2, -2):
                pl.when(there(k))(copy.wait_send)
            else:
                copy.wait_send()
        pl.when(there(-2))(relay_far.wait_send)
        pl.when(there(2))(relay_side.wait_send)
        pl.when(last_there)(relay_last.wait_send)

    return kernel


def solution(mesh):
    blocks = mesh.shape["tok"]

    def on_device(
        tokens, norm_gain, query_weight, w_key, w_value, w_out, head_scale, matching, valid, stops
    ):
        _, rows, width = tokens.shape
        heads = head_scale.shape[0]
        tiles = matching.shape[1]
        slots = 2 * BAND + 1
        table = jnp.asarray(rotary_table(blocks, rows, width // heads))
        vmem = pl.BlockSpec(memory_space=pltpu.VMEM)
        smem = pl.BlockSpec(memory_space=pltpu.SMEM)
        anywhere = pl.BlockSpec(memory_space=pl.ANY)
        square = pltpu.VMEM((width, width), jnp.bfloat16)
        block = pltpu.VMEM((rows, width), jnp.bfloat16)
        band = pltpu.VMEM((slots, rows, width), jnp.bfloat16)
        return pl.pallas_call(
            make_kernel(blocks, rows, width, heads, tiles),
            out_shape=jax.ShapeDtypeStruct(tokens.shape, jnp.bfloat16),
            in_specs=[vmem, vmem, smem, smem, smem, smem] + [anywhere] * 5,
            out_specs=vmem,
            scratch_shapes=[
                square, square, square, square,
                pltpu.VMEM((slots, rows, 2 * LANES), jnp.float32),
                pltpu.VMEM((rows + META, width), jnp.bfloat16),
                pltpu.VMEM((slots, rows + META, width), jnp.bfloat16),
                pltpu.VMEM((8, LANES), jnp.float32),
                pltpu.VMEM((8, LANES), jnp.float32),
                block, band, band,
                pltpu.VMEM((slots, 8, rows), jnp.float32),
                block,
                pltpu.SemaphoreType.DMA((5,)),
                pltpu.SemaphoreType.DMA((7,)),
                pltpu.SemaphoreType.DMA((slots,)),
                pltpu.SemaphoreType.DMA((2,)),
            ],
            compiler_params=pltpu.CompilerParams(
                collective_id=0, has_side_effects=True, vmem_limit_bytes=60 * 1024 * 1024
            ),
            cost_estimate=pl.CostEstimate(
                flops=40 * rows * width * width, bytes_accessed=8 * width * width,
                transcendentals=heads * rows * rows * 4,
            ),
        )(
            tokens, norm_gain[None, :], head_scale, matching, valid, stops,
            query_weight, w_key, w_value, w_out, table,
        )

    in_specs = (
        P("ep", ("grp", "tok"), None),
        P(), P(), P(), P(), P(), P(),
        P("ep", ("grp", "tok")),
        P("ep", ("grp", "tok")),
        P("ep", ("grp", "tok"), None),
    )
    out_specs = P("ep", ("grp", "tok"), None)
    return jax.shard_map(
        on_device, mesh=mesh, in_specs=in_specs, out_specs=out_specs, check_vma=False
    )
```

profile of v0, /device:TPU:6, one launch (start us, length us, event | category | flops | bytes accessed | tf_op | source)
XLA Modules:
  0.0 30.4 jit_solution(3025746775736656629)
XLA Ops:
  0.0 1.3 %broadcast_in_dim.3.gain_ref = f32[1,768]{1,0:T(1,128)} reshape(f32[768]{0:T(1024)} %param.12) | data formatting | bytes 6144 | tf_op jit(solution)/shard_map/broadcast_in_dim | solution.py:341
  1.3 27.5 %shard_map.109 = bf16[1,128,768]{2,1,0:T(8,128)(2,1)} custom-call(bf16[1,128,768]{2,1,0:T(8,128)(2,1)} %tok_ref.1, f32[1,768]{1,0:T(1,128)} %broadcast_in_dim.3.gain_ref, f32[12]{0:T(128)} %scale_ref.1, s32[1,4]{1,0:T(1,128)} %match_ref.1, s32[1,4]{1,0:T(1,128)} %valid_ref.1, s32[1,1,4]{2,1,0:T(1,128)} %stops_ref.1, bf16[768,768]{1,0:T(8,128)(2,1)} %wq_hbm.1, ...), custom_call_target="tpu_custom_call" | custom-call | flops 3019898880 | bytes 4718592 | tf_op jit(solution)/shard_map/pallas_call | solution.py:313
  28.8 1.6 %copy.13 = bf16[1,128,768]{2,1,0:T(8,128)(2,1)} copy(bf16[1,128,768]{2,1,0:T(8,128)(2,1)} %shard_map.109) | data formatting | bytes 393216
where the time goes:
time: 30.6 us; the launch traced here: 30.4 us
  Pallas kernels  27.5 us (90%)
  local copies, waits for them, and re-layouts  2.88 us (9%)
    pallas_call x1, Pallas kernels, on_device(): pl.pallas_call(make_kernel(blocks, rows, width, heads, tiles), out_shape=...  27.5 us
    unnamed x1, local copies, waits for them, and re-layouts  1.62 us
    broadcast_in_dim x1, local copies, waits for them, and re-layouts, on_device(): norm_gain[None, :]  1.27 us

commit v1 on v0

--- a/solution.py
+++ b/solution.py
@@ -51,7 +51,7 @@
         wq_hbm, wk_hbm, wv_hbm, wo_hbm, table_hbm,
         out_ref,
         wq, wk, wv, wo, table, mine, buf, match_out, match_in,
-        queries, keys, values, masks, attended,
+        queries, keys, values, masks, attended, best_ref, total_ref, accum,
         local_sem, send_sem, recv_sem, match_sem,
     ):
         t = lax.axis_index("tok")
@@ -97,7 +97,7 @@
         center = jnp.mean(floated, axis=-1, keepdims=True)
         apart = floated - center
         spread = jnp.mean(apart * apart, axis=-1, keepdims=True)
-        mine[:rows, :] = (apart * lax.rsqrt(spread + 1e-05) * gain_ref[...]).astype(jnp.bfloat16)
+        mine[:rows, :] = (apart * lax.rsqrt(spread + 1e-05) * gain_ref[...].reshape(1, width)).astype(jnp.bfloat16)
 
         row = lax.broadcasted_iota(jnp.int32, (8, LANES), 0)
         matched = jnp.zeros((8, LANES), jnp.float32)
@@ -117,11 +117,18 @@
         )
         swap.start()
 
-        def transfer(src, number, slot, tok, e):
+        cuts = (pl.ds(0, rows // 2), pl.ds(rows // 2, rows // 2 + META))
+
+        def piece(src, number, slot, tok, e, half):
+            cut = cuts[half]
             return pltpu.make_async_remote_copy(
-                src, buf.at[slot], send_sem.at[number], recv_sem.at[slot],
+                src.at[cut], buf.at[slot, cut],
+                send_sem.at[number, half], recv_sem.at[slot, half],
                 device_id={"tok": tok, "ep": e}, device_id_type=MESH,
             )
+
+        def transfer(src, number, slot, tok, e):
+            return [piece(src, number, slot, tok, e, half) for half in range(len(cuts))]
 
         mid = BAND
         direct = [
@@ -135,17 +142,22 @@
         relay_last = transfer(buf.at[mid - s], 6, mid - 3 * s, t + 2 * s, ep)
         last_there = there(2) & there(-1)
 
-        def arrived(k):
-            transfer(mine, 0, mid + s * k, t + s, other_ep).wait_recv()
+        def arrived(k, half):
+            piece(mine, 0, mid + s * k, t + s, other_ep, half).wait_recv()
+
+        def both(k):
+            arrived(k, 0)
+            arrived(k, 1)
 
         mine[rows:, :] = jnp.zeros((META, width), jnp.bfloat16)
         swap.wait_recv()
         mine[rows:, :LANES] = jnp.concatenate([match_in[...], hidden], axis=0).astype(jnp.bfloat16)
-        for k, copy in direct:
-            if k in (2, -2):
-                pl.when(there(k))(copy.start)
-            else:
-                copy.start()
+        for half in range(2):
+            for k, copy in direct:
+                if k in (2, -2):
+                    pl.when(there(k))(copy[half].start)
+                else:
+                    copy[half].start()
 
         loads[0].wait()
         loads[1].wait()
@@ -193,84 +205,115 @@
                     source, wv[:, wide], preferred_element_type=jnp.float32
                 ).astype(jnp.bfloat16)
 
-        arrived(0)
+        def pass_on(half):
+            arrived(1, half)
+            pl.when(there(-2))(relay_far[half].start)
+
+            @pl.when(there(2))
+            def _():
+                arrived(2, half)
+                relay_side[half].start()
+
+        def pass_last(half):
+            @pl.when(there(-1))
+            def _():
+                arrived(-1, half)
+
+            pl.when(last_there)(relay_last[half].start)
+
+        pass_on(0)
+        both(0)
         project(0)
-        arrived(1)
-        pl.when(there(-2))(relay_far.start)
-
-        @pl.when(there(2))
-        def _():
-            arrived(2)
-            relay_side.start()
-
+        pass_on(1)
         project(1)
-
-        @pl.when(there(-2))
-        def _():
-            arrived(-2)
 
         @pl.when(there(2))
         def _():
             project(2)
 
-        @pl.when(there(-1))
-        def _():
-            arrived(-1)
-
-        pl.when(last_there)(relay_last.start)
+        pass_last(0)
 
         @pl.when(there(-2))
         def _():
+            both(-2)
             project(-2)
+
+        pass_last(1)
 
         @pl.when(there(-1))
         def _():
             project(-1)
 
+        ranks = []
+        for i in range(stops_ref.shape[2]):
+            away = jnp.clip(stops_ref[0, 0, i] - t, -BAND, BAND)
+            ranks.append(2 * jnp.abs(away) + (away > 0).astype(jnp.int32))
+        for low, high in ((0, 1), (2, 3), (0, 2), (1, 3), (1, 2)):
+            ranks[low], ranks[high] = (
+                jnp.minimum(ranks[low], ranks[high]), jnp.maximum(ranks[low], ranks[high])
+            )
+        order = [BAND + jnp.where(r % 2 == 1, r // 2, -(r // 2)) for r in ranks]
+        lane_of = lax.broadcasted_iota(jnp.int32, (rows, LANES), 1)
+
+        def attend(picks, first):
+            mask = jnp.concatenate([masks[p][0:1, :] for p in picks], axis=1)
+            for c in range(chunks):
+                span = pl.ds(c * LANES, LANES)
+                ask = queries[:, span]
+                nothing = jnp.zeros_like(ask)
+                asked = jnp.concatenate(
+                    [jnp.where(lane_of // head_dim == h, ask, nothing) for h in range(per_chunk)],
+                    axis=0,
+                )
+                key_use = jnp.concatenate([keys[p, :, span] for p in picks], axis=0)
+                value_use = jnp.concatenate([values[p, :, span] for p in picks], axis=0)
+                raw = lax.dot_general(
+                    asked, key_use, (((1,), (1,)), ((), ())), preferred_element_type=jnp.float32
+                )
+                weights, totals, decays = [], [], []
+                for h in range(per_chunk):
+                    head = c * per_chunk + h
+                    factor = scale_ref[head] * jnp.float32(LOG2E / math.sqrt(head_dim))
+                    scores = raw[h * rows : (h + 1) * rows] * factor + mask
+                    best = jnp.max(scores, axis=1, keepdims=True)
+                    if not first:
+                        before = best_ref[head, :, :1]
+                        best = jnp.maximum(best, before)
+                        decays.append(jnp.exp2(before - best))
+                    weight = jnp.exp2(scores - best)
+                    total = jnp.sum(weight, axis=1, keepdims=True)
+                    if first:
+                        best_ref[head] = jnp.broadcast_to(best, (rows, LANES))
+                        total_ref[head] = jnp.broadcast_to(total, (rows, LANES))
+                    else:
+                        total = total + total_ref[head, :, :1] * decays[h]
+                    totals.append(total)
+                    weights.append(weight.astype(jnp.bfloat16))
+                summed = jnp.dot(
+                    jnp.concatenate(weights, axis=0), value_use, preferred_element_type=jnp.float32
+                )
+                parts = []
+                for h in range(per_chunk):
+                    part = summed[h * rows : (h + 1) * rows]
+                    if not first:
+                        part = (part + accum[:, span] * decays[h]) / totals[h]
+                    parts.append(part)
+                result = parts[0]
+                for h in range(1, per_chunk):
+                    result = jnp.where(lane_of // head_dim == h, parts[h], result)
+                if first:
+                    accum[:, span] = result
+                else:
+                    attended[:, span] = result.astype(jnp.bfloat16)
+
+        attend(order[: BAND - 1], True)
         for k in (3, -3):
             @pl.when(there(k))
             def _():
-                arrived(k)
+                both(k)
                 project(k)
 
-        picks = [
-            jnp.clip(stops_ref[0, 0, i] - t + BAND, 0, slots - 1) for i in range(stops_ref.shape[2])
-        ]
-        mask = jnp.concatenate([masks[p][0:1, :] for p in picks], axis=1)
-        lane_of = lax.broadcasted_iota(jnp.int32, (rows, LANES), 1)
-        for c in range(chunks):
-            span = pl.ds(c * LANES, LANES)
-            ask = queries[:, span]
-            nothing = jnp.zeros_like(ask)
-            asked = jnp.concatenate(
-                [
-                    jnp.where(lane_of // head_dim == h, ask, nothing)
-                    for h in range(per_chunk)
-                ],
-                axis=0,
-            )
-            key_use = jnp.concatenate([keys[p, :, span] for p in picks], axis=0)
-            value_use = jnp.concatenate([values[p, :, span] for p in picks], axis=0)
-            raw = lax.dot_general(
-                asked, key_use, (((1,), (1,)), ((), ())), preferred_element_type=jnp.float32
-            )
-            weights, totals = [], []
-            for h in range(per_chunk):
-                factor = scale_ref[c * per_chunk + h] * jnp.float32(LOG2E / math.sqrt(head_dim))
-                scores = raw[h * rows : (h + 1) * rows] * factor + mask
-                best = jnp.max(scores, axis=1, keepdims=True)
-                weight = jnp.exp2(scores - best)
-                totals.append(jnp.sum(weight, axis=1, keepdims=True))
-                weights.append(weight.astype(jnp.bfloat16))
-            summed = jnp.dot(
-                jnp.concatenate(weights, axis=0), value_use, preferred_element_type=jnp.float32
-            )
-            result = summed[:rows] / totals[0]
-            for h in range(1, per_chunk):
-                result = jnp.where(
-                    lane_of // head_dim == h, summed[h * rows : (h + 1) * rows] / totals[h], result
-                )
-            attended[:, span] = result.astype(jnp.bfloat16)
+        attend(order[BAND - 1 :], False)
 
         loads[4].wait()
         for pair in range(0, chunks, 2):
@@ -281,14 +324,15 @@
             ).astype(jnp.bfloat16)
 
         swap.wait_send()
-        for k, copy in direct:
-            if k in (2, -2):
-                pl.when(there(k))(copy.wait_send)
-            else:
-                copy.wait_send()
-        pl.when(there(-2))(relay_far.wait_send)
-        pl.when(there(2))(relay_side.wait_send)
-        pl.when(last_there)(relay_last.wait_send)
+        for half in range(2):
+            for k, copy in direct:
+                if k in (2, -2):
+                    pl.when(there(k))(copy[half].wait_send)
+                else:
+                    copy[half].wait_send()
+            pl.when(there(-2))(relay_far[half].wait_send)
+            pl.when(there(2))(relay_side[half].wait_send)
+            pl.when(last_there)(relay_last[half].wait_send)
 
     return kernel
 
@@ -325,9 +369,12 @@
                 block, band, band,
                 pltpu.VMEM((slots, 8, rows), jnp.float32),
                 block,
+                pltpu.VMEM((heads, rows, LANES), jnp.float32),
+                pltpu.VMEM((heads, rows, LANES), jnp.float32),
+                pltpu.VMEM((rows, width), jnp.float32),
                 pltpu.SemaphoreType.DMA((5,)),
-                pltpu.SemaphoreType.DMA((7,)),
-                pltpu.SemaphoreType.DMA((slots,)),
+                pltpu.SemaphoreType.DMA((7, 2)),
+                pltpu.SemaphoreType.DMA((slots, 2)),
                 pltpu.SemaphoreType.DMA((2,)),
             ],
             compiler_params=pltpu.CompilerParams(
@@ -338,7 +385,7 @@
                 transcendentals=heads * rows * rows * 4,
             ),
         )(
-            tokens, norm_gain[None, :], head_scale, matching, valid, stops,
+            tokens, norm_gain, head_scale, matching, valid, stops,
             query_weight, w_key, w_value, w_out, table,
         )
 

time: 30.6 us -> 27.6 us (0.902)
  Pallas kernels: 27.5 us -> 25.9 us
  local copies, waits for them, and re-layouts: 2.88 us -> 1.62 us
    pallas_call x1, Pallas kernels: 27.5 us -> 25.9 us  [on_device(): pl.pallas_call(make_kernel(blocks, rows, width, heads, tiles), out_shape=...]
    broadcast_in_dim x1 -> x0, local copies, waits for them, and re-layouts: 1.27 us -> none  [on_device(): norm_gain[None, :]]
where the time goes in v1:
time: 27.6 us; the launch traced here: 27.5 us
  Pallas kernels  25.9 us (94%)
  local copies, waits for them, and re-layouts  1.62 us (6%)
    pallas_call x1, Pallas kernels, on_device(): pl.pallas_call(make_kernel(blocks, rows, width, heads, tiles), out_shape=...  25.9 us
    unnamed x1, local copies, waits for them, and re-layouts  1.62 us

profile of v1, /device:TPU:6, one launch (start us, length us, event | category | flops | bytes accessed | tf_op | source)
XLA Modules:
  0.0 27.5 jit_solution(18424570731535749466)
XLA Ops:
  0.0 25.9 %shard_map.109 = bf16[1,128,768]{2,1,0:T(8,128)(2,1)} custom-call(bf16[1,128,768]{2,1,0:T(8,128)(2,1)} %tok_ref.1, f32[768]{0:T(1024)} %gain_ref.1, f32[12]{0:T(128)} %scale_ref.1, s32[1,4]{1,0:T(1,128)} %match_ref.1, s32[1,4]{1,0:T(1,128)} %valid_ref.1, s32[1,1,4]{2,1,0:T(1,128)} %stops_ref.1, bf16[768,768]{1,0:T(8,128)(2,1)} %wq_hbm.1, ...), custom_call_target="tpu_custom_call" | custom-call | flops 3019898880 | bytes 4718592 | tf_op jit(solution)/shard_map/pallas_call | solution.py:357
  25.9 1.6 %copy.13 = bf16[1,128,768]{2,1,0:T(8,128)(2,1)} copy(bf16[1,128,768]{2,1,0:T(8,128)(2,1)} %shard_map.109) | data formatting | bytes 393216

commit v2 on v1

--- a/solution.py
+++ b/solution.py
@@ -149,15 +149,18 @@
             arrived(k, 0)
             arrived(k, 1)
 
-        mine[rows:, :] = jnp.zeros((META, width), jnp.bfloat16)
-        swap.wait_recv()
-        mine[rows:, :LANES] = jnp.concatenate([match_in[...], hidden], axis=0).astype(jnp.bfloat16)
-        for half in range(2):
+        def send(half):
             for k, copy in direct:
                 if k in (2, -2):
                     pl.when(there(k))(copy[half].start)
                 else:
                     copy[half].start()
+
+        send(0)
+        mine[rows:, :] = jnp.zeros((META, width), jnp.bfloat16)
+        swap.wait_recv()
+        mine[rows:, :LANES] = jnp.concatenate([match_in[...], hidden], axis=0).astype(jnp.bfloat16)
+        send(1)
 
         loads[0].wait()
         loads[1].wait()

time: 27.6 us -> 26.5 us (0.960)
  Pallas kernels: 25.9 us -> 24.7 us
    pallas_call x1, Pallas kernels: 25.9 us -> 24.7 us  [on_device(): pl.pallas_call(make_kernel(blocks, rows, width, heads, tiles), out_shape=...]
where the time goes in v2:
time: 26.5 us; the launch traced here: 26.3 us
  Pallas kernels  24.7 us (93%)
  local copies, waits for them, and re-layouts  1.62 us (6%)
    pallas_call x1, Pallas kernels, on_device(): pl.pallas_call(make_kernel(blocks, rows, width, heads, tiles), out_shape=...  24.7 us
    unnamed x1, local copies, waits for them, and re-layouts  1.62 us

profile of v2, /device:TPU:6, one launch (start us, length us, event | category | flops | bytes accessed | tf_op | source)
XLA Modules:
  0.0 26.3 jit_solution(5581087380115866389)
XLA Ops:
  0.0 24.7 %shard_map.109 = bf16[1,128,768]{2,1,0:T(8,128)(2,1)} custom-call(bf16[1,128,768]{2,1,0:T(8,128)(2,1)} %tok_ref.1, f32[768]{0:T(1024)} %gain_ref.1, f32[12]{0:T(128)} %scale_ref.1, s32[1,4]{1,0:T(1,128)} %match_ref.1, s32[1,4]{1,0:T(1,128)} %valid_ref.1, s32[1,1,4]{2,1,0:T(1,128)} %stops_ref.1, bf16[768,768]{1,0:T(8,128)(2,1)} %wq_hbm.1, ...), custom_call_target="tpu_custom_call" | custom-call | flops 3019898880 | bytes 4718592 | tf_op jit(solution)/shard_map/pallas_call | solution.py:360
  24.7 1.6 %copy.13 = bf16[1,128,768]{2,1,0:T(8,128)(2,1)} copy(bf16[1,128,768]{2,1,0:T(8,128)(2,1)} %shard_map.109) | data formatting | bytes 393216
